TPU v7x, 256 devices: a whole 4x4x8 slice. The times are simulated.
256 devices in a mesh: row: 32 (over z_hi, y, core), col: 8 (over z_lo, x).
Axes of the slice: x: 4, y: 4, z: 8 (z_hi: 4, z_lo: 2; z = z_hi * 2 + z_lo), core: 2. Of those that a mesh axis runs over, the one named last changes fastest.
Arguments:
- window: float32 [16384, 8192], P('row', 'col'), may hold values from -6 to 6
- left_slots: float32 [32, 8, 2, 1, 512, 512], P('row', 'col'), may hold values from -0.25 to 0.25
- right_slots: float32 [32, 8, 2, 2, 512, 512], P('row', 'col'), may hold values from -0.25 to 0.25
- left_owner: int32 [32, 2], P('row'), may hold values from 0 to 7
- right_owner: int32 [8, 2], P('col'), may hold values from 0 to 31
Outputs:
- updated: float32 [16384, 8192], P('row', 'col')
Inputs may be any that keep to these rules, and one draw needn't show every extreme that they name: Only the slot of the device at tile row i and tile column left_owner[i, s] is read for section s of tile row i. Only the slot of the device at tile row right_owner[j, s] and tile column j is read for section s of tile column j.
All inputs are finite; a program needn't handle non-finite values.
Results may differ from a plain program's by a relative error of at most 0.000071.
Values sent between devices are 32-bit elements; how exact they have to be, the bound alone decides.
A program may use at most 64 MiB of HBM per device.

v0:
```python
import jax
import jax.numpy as jnp
from jax import lax
from jax.sharding import PartitionSpec as P

full_precision = lax.Precision.HIGHEST


def spread(block, axis, source):
    block = jnp.where(lax.axis_index(axis) == source, block, jnp.zeros_like(block))
    return lax.psum(block, axis)


def shifted(block, axis, distance):
    devices = range(lax.axis_size(axis))
    route = [(i - distance, i) for i in devices if i - distance in devices]
    return lax.ppermute(block, axis, route)


def left_apply(factors, blocks):
    return jnp.einsum("mkr,mkc->mrc", factors, blocks, precision=full_precision)


def right_apply(blocks, factors):
    return jnp.einsum("rmk,mkc->rmc", blocks, factors, precision=full_precision)


def shards(window, left_slots, right_slots, left_owner, right_owner):
    tile_rows, tile_cols = window.shape
    factor_order = left_slots.shape[-1]
    half_order = factor_order // 2
    left_count = tile_rows // factor_order
    right_count = tile_cols // factor_order
    row_index = lax.axis_index("row")
    col_index = lax.axis_index("col")
    row_first = row_index == 0
    row_final = row_index == lax.axis_size("row") - 1
    col_first = col_index == 0
    col_final = col_index == lax.axis_size("col") - 1
    first_left = spread(left_slots[0, 0, 0], "col", left_owner[0, 0])
    current = left_apply(first_left, window.reshape(left_count, factor_order, tile_cols)).reshape(
        tile_rows, tile_cols
    )
    second_left = spread(left_slots[0, 0, 1], "col", left_owner[0, 1])
    own_top = current[:half_order]
    own_bottom = current[tile_rows - half_order :]
    border_factor = second_left[left_count - 1]
    beneath = shifted(own_top, "row", -1)
    joined = jnp.concatenate([own_bottom, beneath], 0)
    blended = left_apply(border_factor[None], joined[None])[0]
    blended = jnp.where(row_final, joined, blended)
    sent_back = shifted(blended[half_order:], "row", 1)
    new_top = jnp.where(row_first, own_top, sent_back)
    new_bottom = blended[:half_order]
    pieces = [new_top]
    pieces.append(new_bottom)
    current = jnp.concatenate(pieces, 0)
    first_right = spread(right_slots[0, 0, 0], "row", right_owner[0, 0])
    current = right_apply(
        current.reshape(tile_rows, right_count, factor_order), first_right
    ).reshape(tile_rows, tile_cols)
    second_right = spread(right_slots[0, 0, 1], "row", right_owner[0, 1])
    own_left = current[:, :half_order]
    own_right = current[:, tile_cols - half_order :]
    edge_factor = second_right[right_count - 1]
    beside = shifted(own_left, "col", -1)
    joined = jnp.concatenate([own_right, beside], 1)
    blended = right_apply(joined[:, None, :], edge_factor[None])[:, 0]
    blended = jnp.where(col_final, joined, blended)
    sent_back = shifted(blended[:, half_order:], "col", 1)
    new_left = jnp.where(col_first, own_left, sent_back)
    new_right = blended[:, :half_order]
    pieces = [new_left]
    inside = current[:, half_order : tile_cols - half_order].reshape(
        tile_rows, right_count - 1, factor_order
    )
    pieces.append(right_apply(inside, second_right[: right_count - 1]).reshape(tile_rows, -1))
    pieces.append(new_right)
    return jnp.concatenate(pieces, 1)


def solution(mesh):
    in_specs = (
        P("row", "col"),
        P("row", "col", None, None, None, None),
        P("row", "col", None, None, None, None),
        P("row", None),
        P("col", None),
    )
    out_specs = P("row", "col")
    return jax.shard_map(shards, mesh=mesh, in_specs=in_specs, out_specs=out_specs, check_vma=False)
```

profile of v0, /device:TPU:1, one launch (start us, length us, event | category | flops | bytes accessed | tf_op | source)
XLA Modules:
  0.0 470.8 jit_solution(2112989853722655976)
XLA Ops:
  6.5 1.4 fusion.15
  9.2 3.2 select_bitcast_fusion.3
  12.5 0.6 copy-done.3
  14.8 4.7 fusion.10
  19.5 3.0 copy.10
  22.5 2.9 copy.11
  25.4 2.6 select_bitcast_fusion
  27.9 72.2 %all-reduce.7.cloned.1.call-done = (f32[512,512]{1,0:T(8,128)}, f32[512,512]{1,0:T(8,128)}) async-done(((f32[512,512]{1,0:T(8,128)}, f32[512,512]{1,0:T(8,128)}), (f32[512,512]{1,0:T(8,128)}, f32[512,512]{1,0:T(8,128)})) %all-reduce.7.cloned.1.call-update) | async-done | bytes 2097168 | tf_op jit(solution)/shard_map/psum | solution.py:11
  100.2 4.7 %fusion.17 = f32[512,1024]{1,0:T(8,128)S(1)} fusion(f32[512,512]{1,0:T(8,128)} %get-tuple-element.8, f32[512,1024]{1,0:T(8,128)S(1)} %copy-done), kind=kOutput, calls=%fused_computation.31 | convolution fusion | flops 3221225472 | bytes 5242880 | tf_op jit(solution)/shard_map/mkr,mkc->mrc/dot_general | solution.py:21
  104.9 1.3 fusion.13
  106.6 6.6 %collective-permute-start = (f32[256,1024]{1,0:T(8,128)}, f32[256,1024]{1,0:T(8,128)}, u32[]{:S(2)}, u32[]{:S(2)}) collective-permute-start(f32[256,1024]{1,0:T(8,128)} %get-tuple-element.16), channel_id=1, source_target_pairs={{8,0},{16,8},{24,16},{32,24},{40,32},{48,40},{56,48},{64,56},{72,6... | collective-permute-start | bytes 3145736 | tf_op jit(solution)/shard_map/ppermute | solution.py:17
  113.2 16.0 %collective-permute-done = f32[256,1024]{1,0:T(8,128)} collective-permute-done((f32[256,1024]{1,0:T(8,128)}, f32[256,1024]{1,0:T(8,128)}, u32[]{:S(2)}, u32[]{:S(2)}) %collective-permute-start) | collective-permute-done | bytes 1048608 | tf_op jit(solution)/shard_map/ppermute | solution.py:17
  129.2 5.4 %convolution_select_fusion = f32[512,1024]{1,0:T(8,128)S(1)} fusion(f32[512,512]{1,0:T(8,128)} %get-tuple-element.7, f32[256,1024]{1,0:T(8,128)} %collective-permute-done, f32[256,1024]{1,0:T(8,128)S(1)} %get-tuple-element.15, pred[]{:T(512)S(6)} %eq.28), kind=kOutput, calls=%fused_computation.8 | convolution fusion | flops 3222798336 | bytes 5242881 | tf_op jit(solution)/shard_map/mkr,mkc->mrc/dot_general | solution.py:21
  134.7 1.1 fusion.12
  135.8 2.1 collective-permute-start.1
  137.9 13.7 %collective-permute-done.1 = f32[256,1024]{1,0:T(8,128)} collective-permute-done((f32[256,1024]{1,0:T(8,128)}, f32[256,1024]{1,0:T(8,128)}, u32[]{:S(2)}, u32[]{:S(2)}) %collective-permute-start.1) | collective-permute-done | bytes 1048608 | tf_op jit(solution)/shard_map/ppermute | solution.py:17
  151.6 1.7 broadcast_select_fusion
  153.3 1.5 pad_maximum_fusion.1
  154.8 265.2 %all-reduce.5.cloned.1.call-done = (f32[2,512,512]{1,2,0:T(8,128)}, f32[2,512,512]{1,2,0:T(8,128)}) async-done(((f32[2,512,512]{1,2,0:T(8,128)}, f32[2,512,512]{1,2,0:T(8,128)}), (f32[2,512,512]{1,2,0:T(8,128)}, f32[2,512,512]{1,2,0:T(8,128)})) %all-reduce.5.cloned.1.call-update) | async-done | bytes 4194320 | tf_op jit(solution)/shard_map/psum | solution.py:11
  420.0 5.8 %fusion = f32[2,512,512]{2,1,0:T(8,128)S(1)} fusion(f32[2,512,512]{1,2,0:T(8,128)} %get-tuple-element.6, f32[64,2,8,512]{3,2,1,0:T(8,128)} %bitcast.46), kind=kOutput, calls=%fused_computation | convolution fusion | flops 3221225472 | bytes 6291456 | tf_op jit(solution)/shard_map/rmk,mkc->rmc/dot_general | solution.py:25
  425.8 1.3 copy-done.2
  427.1 0.9 fusion.11
  428.0 1.3 collective-permute-start.2
  429.3 13.0 %collective-permute-done.2 = f32[512,256]{0,1:T(8,128)S(1)} collective-permute-done((f32[512,256]{0,1:T(8,128)}, f32[512,256]{0,1:T(8,128)S(1)}, u32[]{:S(2)}, u32[]{:S(2)}) %collective-permute-start.2) | collective-permute-done | bytes 524320 | tf_op jit(solution)/shard_map/ppermute | solution.py:17
  442.3 3.1 fusion.3
  445.4 0.9 fusion.14
  446.3 2.9 collective-permute-start.3
  449.2 3.4 convolution_bitcast_fusion
  452.6 5.9 %collective-permute-done.3 = f32[512,256]{0,1:T(8,128)S(1)} collective-permute-done((f32[512,256]{0,1:T(8,128)}, f32[512,256]{0,1:T(8,128)S(1)}, u32[]{:S(2)}, u32[]{:S(2)}) %collective-permute-start.3) | collective-permute-done | bytes 524320 | tf_op jit(solution)/shard_map/ppermute | solution.py:17
  458.5 1.1 broadcast_select_fusion.1
  459.6 1.5 pad_maximum_fusion.2
  461.1 2.9 copy.9
  (11 shorter events, 1.0 us)
Async XLA Ops:
  6.5 93.7 %copy-start = (f32[512,1024]{1,0:T(8,128)S(1)}, f32[512,1024]{1,0:T(8,128)}, u32[]{:S(2)}) copy-start(f32[512,1024]{1,0:T(8,128)} %param.5) | copy-start | bytes 6291460
  6.5 93.7 %all-reduce.7.cloned.1.call-start = ((), (), s32[]{:S(2)}) async-start(), calls=%async_computation.1 | async-start | bytes 4194304 | tf_op jit(solution)/shard_map/psum | solution.py:11
  12.4 0.7 copy-start.3
  12.4 407.6 %all-reduce.5.cloned.1.call-start = ((), (), s32[]{:S(2)}) async-start(), calls=%async_computation | async-start | bytes 8388608 | tf_op jit(solution)/shard_map/psum | solution.py:11
  104.9 1.7 copy-start.1
  106.6 22.6 %collective-permute-start = (f32[256,1024]{1,0:T(8,128)}, f32[256,1024]{1,0:T(8,128)}, u32[]{:S(2)}, u32[]{:S(2)}) collective-permute-start(f32[256,1024]{1,0:T(8,128)} %get-tuple-element.16), channel_id=1, source_target_pairs={{8,0},{16,8},{24,16},{32,24},{40,32},{48,40},{56,48},{64,56},{72,6... | collective-permute-start | bytes 3145736 | tf_op jit(solution)/shard_map/ppermute | solution.py:17
  135.8 15.8 %collective-permute-start.1 = (f32[256,1024]{1,0:T(8,128)}, f32[256,1024]{1,0:T(8,128)}, u32[]{:S(2)}, u32[]{:S(2)}) collective-permute-start(f32[256,1024]{1,0:T(8,128)} %get-tuple-element.13), channel_id=1, source_target_pairs={{0,8},{8,16},{16,24},{24,32},{32,40},{40,48},{48,56},{56,64},{64,7... | collective-permute-start | bytes 3145736 | tf_op jit(solution)/shard_map/ppermute | solution.py:17
  425.8 1.3 copy-start.2
  428.0 14.3 %collective-permute-start.2 = (f32[512,256]{0,1:T(8,128)}, f32[512,256]{0,1:T(8,128)S(1)}, u32[]{:S(2)}, u32[]{:S(2)}) collective-permute-start(f32[512,256]{0,1:T(8,128)} %get-tuple-element.12), channel_id=1, source_target_pairs={{1,0},{2,1},{3,2},{4,3},{5,4},{6,5},{7,6},{9,8},{10,9},{11,10},{12... | collective-permute-start | bytes 1572872 | tf_op jit(solution)/shard_map/ppermute | solution.py:17
  446.3 12.2 %collective-permute-start.3 = (f32[512,256]{0,1:T(8,128)}, f32[512,256]{0,1:T(8,128)S(1)}, u32[]{:S(2)}, u32[]{:S(2)}) collective-permute-start(f32[512,256]{0,1:T(8,128)} %get-tuple-element.19), channel_id=1, source_target_pairs={{0,1},{1,2},{2,3},{3,4},{4,5},{5,6},{6,7},{8,9},{9,10},{10,11},{11... | collective-permute-start | bytes 1572872 | tf_op jit(solution)/shard_map/ppermute | solution.py:17
Sparse Core Ops, SparseCore 0:
  12.5 87.6 all-reduce.6
  102.9 317.1 all-reduce.4
where the time goes:
time: 475 us; the launch traced here: 471 us
  waiting for transfers between devices  386 us (81%)
  matrix products  22.4 us (5%)
  local copies, waits for them, and re-layouts  21.8 us (5%)
  between operations  16 us (3%)
  starting transfers between devices  12.9 us (3%)
  other arithmetic  11.5 us (2%)
    psum x2, waiting for transfers between devices, spread(): return lax.psum(block, axis)  337 us
    ppermute x4, waiting for transfers between devices, shifted(): return lax.ppermute(block, axis, route)  48.6 us
    ppermute x4, starting transfers between devices, shifted(): return lax.ppermute(block, axis, route)  12.9 us
    dot_general x3, matrix products, right_apply(): return jnp.einsum('rmk,mkc->rmc', blocks, factors, precision=full_precision)  12.2 us
    dot_general x2, matrix products, left_apply(): return jnp.einsum('mkr,mkc->mrc', factors, blocks, precision=full_precision)  10.1 us
  transfers between devices with their start and end apart: 6, of which 6 were waited for; matrix products, arithmetic and copies ran while one was open for 7% of the time, Pallas kernels for 0%

commit v1 on v0

v1 whole, which is shorter than its diff:
```python
import jax
import jax.numpy as jnp
from jax import lax
from jax.experimental import pallas as pl
from jax.experimental.pallas import tpu as pltpu
from jax.sharding import PartitionSpec as P

MESH = pl.DeviceIdType.MESH
F32, BF16 = jnp.float32, jnp.bfloat16
COPIES = 112
PIECE, HALF = 128, 64


def split(value):
    high = value.astype(BF16)
    return high, (value - high.astype(F32)).astype(BF16)


def product(a, b, contract_a=1):
    dims = (((contract_a,), (0,)), ((), ()))

    def dot(p, q):
        return lax.dot_general(p, q, dims, preferred_element_type=F32)

    return dot(a[0], b[0]) + (dot(a[0], b[1]) + dot(a[1], b[0]))


def kernel(
    left_owner, right_owner, window, left, right, out,
    win, left_own, right_own, right_swap, right_pick,
    first_left, second_left, first_right, second_right,
    arrive, merged, home, left_z, right_z, relay, aside,
    win_split, fl_split, sl_split, fr_split, sr_split,
    mid_split, cur, cur_split, above, below, nxt, nxt_split, from_left, from_right,
    result, send_sem, recv_sem, local_sem,
):
    row, col = lax.axis_index("row"), lax.axis_index("col")
    zh, y, core = row // 8, (row // 2) % 4, row % 2
    zl, x = col // 4, col % 4

    def turn(v, d, n=4):
        return lax.rem(v + d + n, n)

    xp, xm = (row, zl * 4 + turn(x, 1)), (row, zl * 4 + turn(x, -1))
    zpair = (row, (1 - zl) * 4 + x)
    yp, ym = (zh * 8 + turn(y, 1) * 2 + core, col), (zh * 8 + turn(y, -1) * 2 + core, col)
    zp, zm = (turn(zh, 1) * 8 + y * 2 + core, col), (turn(zh, -1) * 8 + y * 2 + core, col)
    mate = (zh * 8 + y * 2 + 1 - core, col)
    row_next, row_prev = (turn(row, 1, 32), col), (turn(row, -1, 32), col)
    col_next, col_prev = (row, turn(col, 1, 8)), (row, turn(col, -1, 8))

    loads = []

    def load(src, dst):
        copy = pltpu.make_async_copy(src, dst, local_sem.at[len(loads)])
        copy.start()
        loads.append(copy)
        return copy

    load_left = [load(left.at[0, 0, s, 0], left_own.at[s]) for s in range(2)]
    load_right = [load(right.at[0, 0, s, core], right_own.at[s]) for s in range(2)]
    load_win = load(window, win)

    partners = (xp, xm, zpair, yp, ym, zp, zm, mate, row_next, row_prev, col_next, col_prev)
    barrier = pltpu.get_barrier_semaphore()
    for partner in partners:
        pl.semaphore_signal(barrier, inc=1, device_id=partner, device_id_type=MESH)
    pl.semaphore_wait(barrier, len(partners))

    made = [0]
    sent = []

    def describe(src, dst, device):
        k = made[0]
        made[0] += 1
        return pltpu.make_async_remote_copy(
            src_ref=src, dst_ref=dst, send_sem=send_sem.at[k], recv_sem=recv_sem.at[k],
            device_id=device, device_id_type=MESH,
        )

    def send(src, dst, device):
        copy = describe(src, dst, device)
        copy.start()
        sent.append(copy)
        return copy

    def rows(piece, part=None):
        if part is None:
            return pl.ds(pl.multiple_of(piece * PIECE, PIECE), PIECE)
        return pl.ds(pl.multiple_of(piece * PIECE + part * HALF, HALF), HALF)

    def scatter_start(ref, pos, plus, minus, f):
        far, ahead, behind = turn(pos, 2), turn(pos, 1), turn(pos, -1)
        return (
            send(ref.at[rows(far, 0)], arrive.at[f, 0], plus),
            send(ref.at[rows(far, 1)], arrive.at[f, 1], minus),
            send(ref.at[rows(ahead, 1)], arrive.at[f, 2], plus),
            send(ref.at[rows(behind, 0)], arrive.at[f, 3], minus),
        )

    def scatter_merge(ref, pos, plus, minus, f, owner, copies):
        ahead, behind = turn(pos, 1), turn(pos, -1)
        copies[0].wait_recv()
        merged[f, 0] = jnp.where(owner == behind, arrive[f, 0], ref[rows(ahead, 0), :])
        one = send(merged.at[f, 0], arrive.at[f, 4], plus)
        copies[1].wait_recv()
        merged[f, 1] = jnp.where(owner == ahead, arrive[f, 1], ref[rows(behind, 1), :])
        two = send(merged.at[f, 1], arrive.at[f, 5], minus)
        return copies + (one, two)

    def scatter_end(ref, pos, f, owner, copies):
        ahead, behind = turn(pos, 1), turn(pos, -1)
        for copy in copies[2:]:
            copy.wait_recv()
        low = jnp.where(owner == ahead, arrive[f, 3], arrive[f, 4])
        home[f, :HALF] = jnp.where(owner == pos, ref[rows(pos, 0), :], low)
        high = jnp.where(owner == behind, arrive[f, 2], arrive[f, 5])
        home[f, HALF:] = jnp.where(owner == pos, ref[rows(pos, 1), :], high)

    def gather_start(ref, pos, plus, minus):
        own = ref.at[rows(pos)]
        return (send(own, own, plus), send(own, own, minus))

    def gather_pass(ref, pos, plus, minus, copies):
        ahead, behind = turn(pos, 1), turn(pos, -1)
        copies[0].wait_recv()
        low = ref.at[rows(behind, 0)]
        one = send(low, low, plus)
        copies[1].wait_recv()
        high = ref.at[rows(ahead, 1)]
        return (one, send(high, high, minus))

    def to_mate(ref, where):
        part = ref.at[where]
        return send(part, part, mate)

    swaps = [[], []]

    def swap(s):
        for d in (2, 1, 3, 0):
            where = rows(turn(y, d))
            swaps[s].append(
                send(right.at[0, 0, s, 1 - core, where], right_swap.at[s, where], mate)
            )

    def pick(s, k, own_core):
        where = rows(turn(y, (2, 1, 3, 0)[k]))
        swaps[s][k].wait_recv()
        right_pick[s, where, :] = jnp.where(
            own_core == core, right_own[s, where, :], right_swap[s, where, :]
        )

    lown = [left_owner[0, s] for s in range(2)]
    rown = [right_owner[0, s] for s in range(2)]
    lx, lz = [v % 4 for v in lown], [v // 4 for v in lown]
    ry, rc, rz = [(v // 2) % 4 for v in rown], [v % 2 for v in rown], [v // 8 for v in rown]

    lscatter, rscatter = [None, None], [None, None]
    lsrc = [left.at[0, 0, s, 0] for s in range(2)]
    lval = [left_own.at[s] for s in range(2)]
    rval = [right_pick.at[s] for s in range(2)]

    def left_start(s):
        lscatter[s] = scatter_start(lsrc[s], x, xp, xm, s)

    def left_merge(s):
        load_left[s].wait()
        lscatter[s] = scatter_merge(lval[s], x, xp, xm, s, lx[s], lscatter[s])

    def left_home(s):
        scatter_end(lval[s], x, s, lx[s], lscatter[s])
        return send(home.at[s], left_z.at[s], zpair)

    def right_start(s):
        load_right[s].wait()
        for k in range(3):
            pick(s, k, rc[s])
        rscatter[s] = scatter_start(rval[s], y, yp, ym, 2 + s)
        pick(s, 3, rc[s])

    def right_merge(s):
        rscatter[s] = scatter_merge(rval[s], y, yp, ym, 2 + s, ry[s], rscatter[s])

    def right_home(s):
        scatter_end(rval[s], y, 2 + s, ry[s], rscatter[s])
        return (
            send(home.at[2 + s, pl.ds(0, HALF)], right_z.at[s, 0], zp),
            send(home.at[2 + s, pl.ds(HALF, HALF)], right_z.at[s, 1], zm),
        )

    def right_relay(s, copies):
        copies[0].wait_recv()
        relay[s, 0] = jnp.where(rz[s] == zh, home[2 + s, HALF:], right_z[s, 0])
        one = send(relay.at[s, 0], right_z.at[s, 2], zp)
        copies[1].wait_recv()
        relay[s, 1] = jnp.where(rz[s] == zh, home[2 + s, :HALF], right_z[s, 1])
        return (one, send(relay.at[s, 1], right_z.at[s, 3], zm))

    def right_piece(s, copies):
        for copy in copies:
            copy.wait_recv()
        own, behind, ahead = rz[s] == zh, rz[s] == turn(zh, -1), rz[s] == turn(zh, 1)
        plus_one, minus_one, plus_two, minus_two = (right_z[s, k] for k in range(4))
        low = jnp.where(behind, plus_one, jnp.where(ahead, minus_two, plus_two))
        high = jnp.where(behind, plus_two, jnp.where(ahead, minus_one, minus_two))
        return jnp.where(own, home[2 + s, :HALF], low), jnp.where(own, home[2 + s, HALF:], high)

    def store_split(pair, where, value):
        high, low = split(value)
        pair[(0, *where)] = high
        pair[(1, *where)] = low

    swap(0)
    left_start(0)
    right_start(0)
    swap(1)
    left_merge(0)
    left_start(1)
    right_merge(0)
    load_win.wait()
    store_split(win_split, (slice(None), slice(None)), win[...])
    right_start(1)
    lz1 = left_home(0)
    left_merge(1)
    rz1 = right_home(0)
    right_merge(1)
    lz1.wait_recv()
    first_left[rows(x), :] = jnp.where(lz[0] == zl, home[0], left_z[0])
    lg1 = gather_start(first_left, x, xp, xm)
    rz1 = right_relay(0, rz1)
    lz2 = left_home(1)
    rz2 = right_home(1)
    lf1 = gather_pass(first_left, x, xp, xm, lg1)
    low, high = right_piece(0, rz1)
    mine = first_right.at[core]
    mine[rows(y, 0), :] = low
    mine[rows(y, 1), :] = high
    rg1 = gather_start(mine, y, yp, ym)
    mates1 = [to_mate(mine, rows(y))]
    lz2.wait_recv()
    piece = jnp.where(lz[1] == zl, home[1], left_z[1])
    second_left[rows(x), :256] = piece[:, :256]
    aside[0] = piece[:, 256:]
    shift_left = send(aside.at[0], second_left.at[rows(x), pl.ds(256, 256)], row_next)
    rz2 = right_relay(1, rz2)
    for copy in lf1:
        copy.wait_recv()
    store_split(fl_split, (slice(None), slice(None)), first_left[...])
    shift_left.wait_recv()
    lg2 = gather_start(second_left, x, xp, xm)
    rf1 = gather_pass(mine, y, yp, ym, rg1)
    mates1 += [to_mate(mine, rows(turn(y, -1))), to_mate(mine, rows(turn(y, 1)))]
    for t in range(4):
        cols = slice(t * 256, t * 256 + 256)
        store_split(
            mid_split,
            (slice(None), cols),
            product((fl_split[0], fl_split[1]), (win_split[0, :, cols], win_split[1, :, cols]), 0),
        )
    low, high = right_piece(1, rz2)
    mine2 = second_right.at[core]
    mine2[rows(y, 0), :256] = low[:, :256]
    mine2[rows(y, 1), :256] = high[:, :256]
    aside[1, :HALF] = low[:, 256:]
    aside[1, HALF:] = high[:, 256:]
    shift_right = describe(aside.at[1], second_right.at[1, rows(y), pl.ds(256, 256)], col_next)

    @pl.when(core == 1)
    def _():
        shift_right.start()

    @pl.when(core == 0)
    def _():
        mine2[rows(y), 256:] = aside[1]

    for copy in rf1:
        copy.wait_recv()
    mates1 += [to_mate(mine, rows(turn(y, 2)))]
    lf2 = gather_pass(second_left, x, xp, xm, lg2)

    @pl.when(core == 1)
    def _():
        shift_right.wait_recv()

    rg2 = gather_start(mine2, y, yp, ym)
    mates2 = [to_mate(mine2, rows(y))]
    for copy in mates1:
        copy.wait_recv()
    for m in range(2):
        store_split(fr_split, (m,), first_right[m])

    order = (0, 3, 1, 2)
    row_swaps = [None] * 4
    for t in order:
        m, h = t // 2, t % 2
        cols, band, part = slice(t * 256, t * 256 + 256), slice(m * 512, m * 512 + 512), slice(h * 256, h * 256 + 256)
        value = product(
            (mid_split[0, :, band], mid_split[1, :, band]),
            (fr_split[0, m, :, part], fr_split[1, m, :, part]),
        )
        cur[t] = value
        store_split(cur_split, (t,), value)
        row_swaps[t] = (
            send(cur.at[t, pl.ds(0, 256)], below.at[t], row_prev),
            send(cur.at[t, pl.ds(256, 256)], above.at[t], row_next),
        )
    rf2 = gather_pass(mine2, y, yp, ym, rg2)
    mates2 += [to_mate(mine2, rows(turn(y, -1))), to_mate(mine2, rows(turn(y, 1)))]
    for copy in lf2:
        copy.wait_recv()
    store_split(sl_split, (slice(None), slice(None)), second_left[...])

    top_stays, bottom_stays = row == 0, row == 31
    col_swaps = []
    for t in order:
        for copy in row_swaps[t]:
            copy.wait_recv()
        up, down = split(above[t]), split(below[t])
        top = (cur_split[0, t, :256], cur_split[1, t, :256])
        bottom = (cur_split[0, t, 256:], cur_split[1, t, 256:])

        def factor(k, side):
            at = (slice(k * 256, k * 256 + 256), slice(side * 256, side * 256 + 256))
            return sl_split[(0, *at)], sl_split[(1, *at)]

        new_top = product(factor(0, 1), up, 0) + product(factor(1, 1), top, 0)
        new_bottom = product(factor(0, 0), bottom, 0) + product(factor(1, 0), down, 0)
        new_top = jnp.where(top_stays, cur[t, :256], new_top)
        new_bottom = jnp.where(bottom_stays, cur[t, 256:], new_bottom)
        nxt[t, :256] = new_top
        nxt[t, 256:] = new_bottom
        store_split(nxt_split, (t, slice(0, 256)), new_top)
        store_split(nxt_split, (t, slice(256, 512)), new_bottom)
        if t == 0:
            col_swaps.append(send(nxt.at[0], from_right, col_prev))
        if t == 3:
            col_swaps.append(send(nxt.at[3], from_left, col_next))
        if t == 3:
            for copy in rf2:
                copy.wait_recv()
            mates2 += [to_mate(mine2, rows(turn(y, 2)))]
    for copy in mates2:
        copy.wait_recv()
    for m in range(2):
        store_split(sr_split, (m,), second_right[m])

    def step(t, m, k, side):
        at = (m, slice(k * 256, k * 256 + 256), slice(side * 256, side * 256 + 256))
        return product((nxt_split[0, t], nxt_split[1, t]), (sr_split[(0, *at)], sr_split[(1, *at)]))

    for side in range(2):
        result[:, 256 + side * 256 : 512 + side * 256] = step(1, 0, 0, side) + step(2, 0, 1, side)
    col_swaps[0].wait_recv()
    other = split(from_right[...])
    edge = step(3, 1, 0, 0) + product(other, (sr_split[0, 1, 256:, :256], sr_split[1, 1, 256:, :256]))
    result[:, 768:] = jnp.where(col == 7, nxt[3], edge)
    col_swaps[1].wait_recv()
    other = split(from_left[...])
    edge = step(0, 1, 1, 1) + product(other, (sr_split[0, 1, :256, 256:], sr_split[1, 1, :256, 256:]))
    result[:, :256] = jnp.where(col == 0, nxt[0], edge)
    store = pltpu.make_async_copy(result, out, local_sem.at[len(loads)])
    store.start()
    for copy in sent:
        copy.wait_send()

    @pl.when(core == 1)
    def _():
        shift_right.wait_send()

    store.wait()


def shards(window, left_slots, right_slots, left_owner, right_owner):
    scratch = [
        pltpu.VMEM((512, 1024), F32),
        pltpu.VMEM((2, 512, 512), F32),
        pltpu.VMEM((2, 512, 512), F32),
        pltpu.VMEM((2, 512, 512), F32),
        pltpu.VMEM((2, 512, 512), F32),
        pltpu.VMEM((512, 512), F32),
        pltpu.VMEM((512, 512), F32),
        pltpu.VMEM((2, 512, 512), F32),
        pltpu.VMEM((2, 512, 512), F32),
        pltpu.VMEM((4, 6, HALF, 512), F32),
        pltpu.VMEM((4, 2, HALF, 512), F32),
        pltpu.VMEM((4, PIECE, 512), F32),
        pltpu.VMEM((2, PIECE, 512), F32),
        pltpu.VMEM((2, 4, HALF, 512), F32),
        pltpu.VMEM((2, 2, HALF, 512), F32),
        pltpu.VMEM((2, PIECE, 256), F32),
        pltpu.VMEM((2, 512, 1024), BF16),
        pltpu.VMEM((2, 512, 512), BF16),
        pltpu.VMEM((2, 512, 512), BF16),
        pltpu.VMEM((2, 2, 512, 512), BF16),
        pltpu.VMEM((2, 2, 512, 512), BF16),
        pltpu.VMEM((2, 512, 1024), BF16),
        pltpu.VMEM((4, 512, 256), F32),
        pltpu.VMEM((2, 4, 512, 256), BF16),
        pltpu.VMEM((4, 256, 256), F32),
        pltpu.VMEM((4, 256, 256), F32),
        pltpu.VMEM((4, 512, 256), F32),
        pltpu.VMEM((2, 4, 512, 256), BF16),
        pltpu.VMEM((512, 256), F32),
        pltpu.VMEM((512, 256), F32),
        pltpu.VMEM((512, 1024), F32),
        pltpu.SemaphoreType.DMA((COPIES,)),
        pltpu.SemaphoreType.DMA((COPIES,)),
        pltpu.SemaphoreType.DMA((8,)),
    ]
    smem, hbm = pl.BlockSpec(memory_space=pltpu.SMEM), pl.BlockSpec(memory_space=pl.ANY)
    return pl.pallas_call(
        kernel,
        name="far_update",
        out_shape=jax.ShapeDtypeStruct(window.shape, F32),
        in_specs=[smem, smem, hbm, hbm, hbm],
        out_specs=hbm,
        scratch_shapes=scratch,
        compiler_params=pltpu.CompilerParams(
            collective_id=0, has_side_effects=True, vmem_limit_bytes=58 * 2**20
        ),
    )(left_owner, right_owner, window, left_slots, right_slots)


def solution(mesh):
    in_specs = (
        P("row", "col"),
        P("row", "col", None, None, None, None),
        P("row", "col", None, None, None, None),
        P("row", None),
        P("col", None),
    )
    out_specs = P("row", "col")
    return jax.shard_map(shards, mesh=mesh, in_specs=in_specs, out_specs=out_specs, check_vma=False)
```

time: 475 us -> 107 us (0.23)
  waiting for transfers between devices: 386 us -> 0 us
  Pallas kernels: 0 us -> 104 us
  matrix products: 22.4 us -> 0 us
  local copies, waits for them, and re-layouts: 21.8 us -> 3.16 us
  between operations: 16 us -> 0.01 us
  starting transfers between devices: 12.9 us -> 0 us
  other arithmetic: 11.5 us -> 0 us
    psum x2 -> x0, waiting for transfers between devices: 337 us -> none  [spread(): return lax.psum(block, axis)]
    pallas_call x0 -> x1, Pallas kernels: none -> 104 us  [shards(): pl.pallas_call(kernel, name='far_update', out_shape=jax.ShapeDtypeStruct(...]
    ppermute x4 -> x0, waiting for transfers between devices: 48.6 us -> none  [shifted(): return lax.ppermute(block, axis, route)]
    dot_general x5 -> x0, matrix products: 22.4 us -> none  [the longest x3 12.2 us: right_apply(): return jnp.einsum('rmk,mkc->rmc', blocks, factors, precision=full_precision)]
    ppermute x4 -> x0, starting transfers between devices: 12.9 us -> none  [shifted(): return lax.ppermute(block, axis, route)]
    slice x7 -> x0, local copies, waits for them, and re-layouts: 10.9 us -> none  [the longest x2 5.26 us: shards(): first_right = spread(right_slots[0, 0, 0], 'row', right_owner[0, 0])]
    select_n x3 -> x0, other arithmetic: 5.36 us -> none  [the longest x1 2.56 us: spread(): jnp.where(lax.axis_index(axis) == source, block, jnp.zeros_like(block))]
    unnamed x10 -> x1, local copies, waits for them, and re-layouts: 8.07 us -> 3.16 us
  transfers between devices with their start and end apart: 6 -> 0, of which waited for: 6 -> 0; matrix products, arithmetic and copies ran while one was open for 7% -> 0% of each run, Pallas kernels for 0% -> 0%
where the time goes in v1:
time: 107 us
  Pallas kernels  104 us (97%)
  local copies, waits for them, and re-layouts  3.16 us (3%)
    pallas_call x1, Pallas kernels, shards(): pl.pallas_call(kernel, name='far_update', out_shape=jax.ShapeDtypeStruct(...  104 us
    unnamed x1, local copies, waits for them, and re-layouts  3.16 us

profile of v1, /device:TPU:1, one launch (start us, length us, event | category | flops | bytes accessed | tf_op | source)
XLA Modules:
  0.0 107.0 jit_solution(13964972665733240844)
XLA Ops:
  0.0 103.8 %far_update.1 = f32[512,1024]{1,0:T(8,128)} custom-call(s32[1,2]{1,0:T(1,128)} %left_owner.1, s32[1,2]{1,0:T(1,128)} %right_owner.1, f32[512,1024]{1,0:T(8,128)} %window.1, f32[1,1,2,1,512,512]{5,4,3,2,1,0:T(8,128)} %left.1, f32[1,1,2,2,512,512]{5,4,3,2,1,0:T(8,128)} %right.1), custom_call_target="tpu_custom_call" | custom-call | tf_op jit(solution)/shard_map/far_update/pallas_call | solution.py:411
  103.8 3.2 %copy.7 = f32[512,1024]{1,0:T(8,128)} copy(f32[512,1024]{1,0:T(8,128)} %far_update.1) | data formatting | bytes 4194304

commit v2 on v0

v2 whole, which is shorter than its diff:
```python
import functools

import jax
import jax.numpy as jnp
from jax import lax
from jax.experimental import pallas as pl
from jax.experimental.pallas import tpu as pltpu
from jax.sharding import PartitionSpec as P

MESH = pl.DeviceIdType.MESH
F32, BF16 = jnp.float32, jnp.bfloat16
COPIES = 176
PIECE, HALF = 128, 64
ORDER = (
    "L1a.start", "R1a.swap", "win", "R1b.swap", "R2a.swap", "L1b.start", "R1a.start", "L1a.merge",
    "R1b.start", "L1b.merge", "L1a.home", "L2b.start", "R1a.merge", "L1b.home", "R1b.merge", "R2b.swap",
    "L2a.start", "R1a.home", "R1b.home", "R2a.start", "L2b.merge", "R2b.start", "L1a.piece", "L2b.home",
    "L1b.piece", "R1b.relay", "R2a.merge", "L2a.merge", "R2b.merge", "L1b.pass", "L1a.pass", "R1a.relay",
    "L2b.shift", "R1b.piece", "L2a.home", "L2b.piece", "R2b.home", "R1a.piece", "L1b.done", "R1b.pass",
    "L1a.done", "x1.0", "L2a.piece", "x1.1", "x1.2", "L2a.pass", "R2b.relay", "L2b.pass", "R1a.pass",
    "R1b.last", "hop0", "x1.3", "hop1", "hop2", "R2a.home", "L2a.done", "L2b.done", "R1b.done", "x2.0",
    "R2b.shift", "hop3", "x2.1", "R1a.last", "R2a.relay", "x2.2", "R2b.piece", "R1a.done", "x2.3", "x3.0",
    "R2a.piece", "x3.3", "x3.2", "x3.1", "R2b.pass", "R2a.pass", "R2b.last", "R2a.last", "R2b.done",
    "R2a.done", "mid", "edgeR", "edgeL",
)


def split(value):
    high = value.astype(BF16)
    return high, (value - high.astype(F32)).astype(BF16)


def product(a, b, contract_a=1):
    dims = (((contract_a,), (0,)), ((), ()))

    def dot(p, q):
        return lax.dot_general(p, q, dims, preferred_element_type=F32)

    return dot(a[0], b[0]) + (dot(a[0], b[1]) + dot(a[1], b[0]))


def kernel(
    left_owner, right_owner, window, left, right, out,
    win, left_own, right_own, right_swap, right_pick,
    first_left, second_left, first_right, second_right,
    arrive, merged, home, left_z, right_z, relay, aside,
    win_split, fl_split, sl_split, fr_split, sr_split,
    mid_split, cur, cur_split, above, below, hop, nxt, nxt_split, from_left, from_right,
    result, send_sem, recv_sem, local_sem,
):
    row, col = lax.axis_index("row"), lax.axis_index("col")
    zh, y, core = row // 8, (row // 2) % 4, row % 2
    zl, x = col // 4, col % 4

    def turn(v, d, n=4):
        return lax.rem(v + d + n, n)

    xp, xm = (row, zl * 4 + turn(x, 1)), (row, zl * 4 + turn(x, -1))
    zpair = (row, (1 - zl) * 4 + x)
    yp, ym = (zh * 8 + turn(y, 1) * 2 + core, col), (zh * 8 + turn(y, -1) * 2 + core, col)
    zp, zm = (turn(zh, 1) * 8 + y * 2 + core, col), (turn(zh, -1) * 8 + y * 2 + core, col)
    mate = (zh * 8 + y * 2 + 1 - core, col)
    row_next, row_prev = (turn(row, 1, 32), col), (turn(row, -1, 32), col)
    col_next, col_prev = (row, turn(col, 1, 8)), (row, turn(col, -1, 8))

    loads = []

    def load(src, dst):
        copy = pltpu.make_async_copy(src, dst, local_sem.at[len(loads)])
        copy.start()
        loads.append(copy)
        return copy

    load_left = [load(left.at[0, 0, s, 0], left_own.at[s]) for s in range(2)]
    load_right = [load(right.at[0, 0, s, core], right_own.at[s]) for s in range(2)]
    load_win = load(window, win)
    loaded = []

    def need(copy):
        if not any(copy is other for other in loaded):
            copy.wait()
            loaded.append(copy)

    is_last, is_first = (y == 3) & (core == 1), (y == 0) & (core == 0)
    across = (zh * 8 + 7 - y * 2 - core, col)
    partners = (
        xp, xm, zpair, yp, ym, zp, zm, mate, row_next, row_prev, col_next, col_prev, across,
    )
    barrier = pltpu.get_barrier_semaphore()
    for partner in partners:
        pl.semaphore_signal(barrier, inc=1, device_id=partner, device_id_type=MESH)
    pl.semaphore_wait(barrier, len(partners))

    made = [0]
    sent = []

    def describe(src, dst, device):
        k = made[0]
        made[0] += 1
        return pltpu.make_async_remote_copy(
            src_ref=src, dst_ref=dst, send_sem=send_sem.at[k], recv_sem=recv_sem.at[k],
            device_id=device, device_id_type=MESH,
        )

    def send(src, dst, device):
        copy = describe(src, dst, device)
        copy.start()
        sent.append(copy)
        return copy

    def rows(piece, part=None):
        if part is None:
            return pl.ds(pl.multiple_of(piece * PIECE, PIECE), PIECE)
        return pl.ds(pl.multiple_of(piece * PIECE + part * HALF, HALF), HALF)

    def scatter_start(ref, pos, plus, minus, f):
        far, ahead, behind = turn(pos, 2), turn(pos, 1), turn(pos, -1)
        return (
            send(ref(rows(far, 0)), arrive.at[f, 0], plus),
            send(ref(rows(far, 1)), arrive.at[f, 1], minus),
            send(ref(rows(ahead, 1)), arrive.at[f, 2], plus),
            send(ref(rows(behind, 0)), arrive.at[f, 3], minus),
        )

    def scatter_merge(value, pos, plus, minus, f, owner, copies):
        ahead, behind = turn(pos, 1), turn(pos, -1)
        copies[0].wait_recv()
        merged[f, 0] = jnp.where(owner == behind, arrive[f, 0], value(rows(ahead, 0)))
        one = send(merged.at[f, 0], arrive.at[f, 4], plus)
        copies[1].wait_recv()
        merged[f, 1] = jnp.where(owner == ahead, arrive[f, 1], value(rows(behind, 1)))
        two = send(merged.at[f, 1], arrive.at[f, 5], minus)
        return copies + (one, two)

    def scatter_end(value, pos, f, owner, copies):
        ahead, behind = turn(pos, 1), turn(pos, -1)
        for copy in copies[2:]:
            copy.wait_recv()
        low = jnp.where(owner == ahead, arrive[f, 3], arrive[f, 4])
        home[f, :HALF] = jnp.where(owner == pos, value(rows(pos, 0)), low)
        high = jnp.where(owner == behind, arrive[f, 2], arrive[f, 5])
        home[f, HALF:] = jnp.where(owner == pos, value(rows(pos, 1)), high)

    def gather_start(ref, pos, plus, minus):
        own = ref.at[rows(pos)]
        return (send(own, own, plus), send(own, own, minus))

    def gather_pass(ref, pos, plus, minus, copies):
        ahead, behind = turn(pos, 1), turn(pos, -1)
        copies[0].wait_recv()
        low = ref.at[rows(behind, 0)]
        one = send(low, low, plus)
        copies[1].wait_recv()
        high = ref.at[rows(ahead, 1)]
        return (one, send(high, high, minus))

    def to_mate(ref, where):
        part = ref.at[where]
        return send(part, part, mate)

    def store_split(pair, where, value):
        high, low = split(value)
        pair[(0, *where)] = high
        pair[(1, *where)] = low

    lown = [left_owner[0, s] for s in range(2)]
    rown = [right_owner[0, s] for s in range(2)]
    lx, lz = [v % 4 for v in lown], [v // 4 for v in lown]
    ry, rc, rz = [(v // 2) % 4 for v in rown], [v % 2 for v in rown], [v // 8 for v in rown]
    steps = {}
    at = {}

    def left_unit(s, h, name):
        f, here = s * 2 + h, pl.ds(h * 256, 256)
        place = (first_left, second_left)[s].at[h]
        pair = (fl_split, sl_split)[s]

        def ref(where):
            return left.at[0, 0, s, 0, where, here]

        def value(where):
            return left_own[s, where, here]

        def start():
            at[f] = scatter_start(ref, x, xp, xm, f)

        def merge():
            need(load_left[s])
            at[f] = scatter_merge(value, x, xp, xm, f, lx[s], at[f])

        def end():
            scatter_end(value, x, f, lx[s], at[f])
            at[f] = send(home.at[f], left_z.at[f], zpair)

        def chosen():
            at[f].wait_recv()
            return jnp.where(lz[s] == zl, home[f], left_z[f])

        def shift():
            aside[0] = chosen()
            at[f] = send(aside.at[0], place.at[rows(x)], row_next)

        def piece():
            if (s, h) == (1, 1):
                at[f].wait_recv()
            else:
                place[rows(x), :] = chosen()
            at[f] = gather_start(place, x, xp, xm)

        def forward():
            at[f] = gather_pass(place, x, xp, xm, at[f])

        def done():
            for copy in at[f]:
                copy.wait_recv()
            store_split(pair, (h,), place[...])

        steps.update({
            name + ".start": start, name + ".merge": merge, name + ".home": end, name + ".shift": shift,
            name + ".piece": piece, name + ".pass": forward, name + ".done": done,
        })

    def right_unit(s, h, name):
        f, g, here = 4 + s * 2 + h, s * 2 + h, pl.ds(h * 256, 256)
        both = (first_right, second_right)[s]
        place = both.at[core, h]
        pair = (fr_split, sr_split)[s]
        mates = []

        def ref(where):
            return right_pick.at[g, where]

        def value(where):
            return right_pick[g, where, :]

        def swap():
            at[f] = send(right.at[0, 0, s, 1 - core, :, here], right_swap.at[g], mate)

        def start():
            need(load_right[s])
            at[f].wait_recv()
            right_pick[g] = jnp.where(rc[s] == core, right_own[s, :, here], right_swap[g])
            at[f] = scatter_start(ref, y, yp, ym, f)

        def merge():
            at[f] = scatter_merge(value, y, yp, ym, f, ry[s], at[f])

        def end():
            scatter_end(value, y, f, ry[s], at[f])
            at[f] = (
                send(home.at[f, pl.ds(0, HALF)], right_z.at[g, 0], zp),
                send(home.at[f, pl.ds(HALF, HALF)], right_z.at[g, 1], zm),
            )

        def pass_on():
            one, two = at[f]
            one.wait_recv()
            relay[g, 0] = jnp.where(rz[s] == zh, home[f, HALF:], right_z[g, 0])
            three = send(relay.at[g, 0], right_z.at[g, 2], zp)
            two.wait_recv()
            relay[g, 1] = jnp.where(rz[s] == zh, home[f, :HALF], right_z[g, 1])
            at[f] = (three, send(relay.at[g, 1], right_z.at[g, 3], zm))

        def chosen():
            for copy in at[f]:
                copy.wait_recv()
            own, behind, ahead = rz[s] == zh, rz[s] == turn(zh, -1), rz[s] == turn(zh, 1)
            plus_one, minus_one, plus_two, minus_two = (right_z[g, k] for k in range(4))
            low = jnp.where(behind, plus_one, jnp.where(ahead, minus_two, plus_two))
            high = jnp.where(behind, plus_two, jnp.where(ahead, minus_one, minus_two))
            return jnp.where(own, home[f, :HALF], low), jnp.where(own, home[f, HALF:], high)

        def shift():
            aside[1, :HALF], aside[1, HALF:] = chosen()
            at[f] = describe(aside.at[1], second_right.at[1, 1, rows(y)], col_next)
            at["shift"] = at[f]

            @pl.when(core == 1)
            def _():
                at[f].start()

            @pl.when(core == 0)
            def _():
                place[rows(y), :] = aside[1]

        def piece():
            if (s, h) == (1, 1):

                @pl.when(core == 1)
                def _():
                    at[f].wait_recv()
            else:
                place[rows(y, 0), :], place[rows(y, 1), :] = chosen()
            at[f] = gather_start(place, y, yp, ym)
            mates.append(to_mate(place, rows(y)))

        def forward():
            at[f] = gather_pass(place, y, yp, ym, at[f])
            mates.append(to_mate(place, rows(turn(y, -1))))
            mates.append(to_mate(place, rows(turn(y, 1))))

        def last():
            for copy in at[f]:
                copy.wait_recv()
            mates.append(to_mate(place, rows(turn(y, 2))))

        def done():
            for copy in mates:
                copy.wait_recv()
            for m in range(2):
                store_split(pair, (m, h), both[m, h])

        steps.update({
            name + ".swap": swap, name + ".start": start, name + ".merge": merge, name + ".home": end,
            name + ".relay": pass_on, name + ".shift": shift, name + ".piece": piece, name + ".pass": forward,
            name + ".last": last, name + ".done": done,
        })

    for s in range(2):
        for h in range(2):
            tail = "12"[s] + "ab"[h]
            left_unit(s, h, "L" + tail)
            right_unit(s, h, "R" + tail)

    def border_send(t):
        up, down = cur.at[t, pl.ds(0, 256)], cur.at[t, pl.ds(256, 256)]
        to_prev = describe(up, below.at[t], row_prev)
        to_next = describe(down, above.at[t], row_next)
        last = [
            describe(cur.at[t, pl.ds(256, 128)], hop.at[t, 0], zp),
            describe(cur.at[t, pl.ds(384, 128)], hop.at[t, 1], across),
        ]
        first = [
            describe(cur.at[t, pl.ds(0, 128)], hop.at[t, 0], zm),
            describe(cur.at[t, pl.ds(128, 128)], hop.at[t, 1], across),
        ]
        last_on = [
            describe(hop.at[t, 0], above.at[t, pl.ds(0, 128)], across),
            describe(hop.at[t, 1], below.at[t, pl.ds(128, 128)], zm),
        ]
        first_on = [
            describe(hop.at[t, 0], below.at[t, pl.ds(0, 128)], across),
            describe(hop.at[t, 1], above.at[t, pl.ds(128, 128)], zp),
        ]

        @pl.when(~is_last)
        def _():
            to_next.start()

        @pl.when(~is_first)
        def _():
            to_prev.start()

        @pl.when(is_last)
        def _():
            for copy in last:
                copy.start()

        @pl.when(is_first)
        def _():
            for copy in first:
                copy.start()

        return to_prev, to_next, last, first, last_on, first_on

    def border_pass(copies):
        _, _, last, first, last_on, first_on = copies

        @pl.when(is_last)
        def _():
            last[0].wait_recv()
            last_on[0].start()
            first[1].wait_recv()
            last_on[1].start()

        @pl.when(is_first)
        def _():
            first[0].wait_recv()
            first_on[0].start()
            last[1].wait_recv()
            first_on[1].start()

    def border_wait(copies):
        to_prev, to_next, _, _, last_on, first_on = copies

        @pl.when(~is_last)
        def _():
            to_prev.wait_recv()

        @pl.when(~is_first)
        def _():
            to_next.wait_recv()

        @pl.when(is_last)
        def _():
            first_on[0].wait_recv()
            last_on[1].wait_recv()

        @pl.when(is_first)
        def _():
            last_on[0].wait_recv()
            first_on[1].wait_recv()

    def border_end(copies):
        to_prev, to_next, last, first, last_on, first_on = copies

        @pl.when(~is_last)
        def _():
            to_next.wait_send()

        @pl.when(~is_first)
        def _():
            to_prev.wait_send()

        @pl.when(is_last)
        def _():
            for copy in last + last_on:
                copy.wait_send()

        @pl.when(is_first)
        def _():
            for copy in first + first_on:
                copy.wait_send()

    top_stays, bottom_stays = row == 0, row == 31
    row_swaps, col_swaps = {}, {}

    def win_step():
        need(load_win)
        store_split(win_split, (slice(None), slice(None)), win[...])

    def first_rows(t):
        cols = slice(t * 256, t * 256 + 256)
        for h in range(2):
            part = slice(h * 256, h * 256 + 256)
            value = product(
                (fl_split[0, h], fl_split[1, h]), (win_split[0, :, cols], win_split[1, :, cols]), 0
            )
            cur[t, part] = value
            store_split(cur_split, (t, part), value)
        row_swaps[t] = border_send(t)

    def second_rows(t):
        border_wait(row_swaps[t])
        cols = slice(t * 256, t * 256 + 256)
        top = (cur_split[0, t, :256], cur_split[1, t, :256])
        bottom = (cur_split[0, t, 256:], cur_split[1, t, 256:])

        def blend(h, upper, lower):
            one = product((sl_split[0, h, :256], sl_split[1, h, :256]), upper, 0)
            return one + product((sl_split[0, h, 256:], sl_split[1, h, 256:]), lower, 0)

        new_bottom = blend(0, bottom, split(below[t]))
        new_top = blend(1, split(above[t]), top)
        new_top = jnp.where(top_stays, cur[t, :256], new_top)
        new_bottom = jnp.where(bottom_stays, cur[t, 256:], new_bottom)
        store_split(mid_split, (slice(0, 256), cols), new_top)
        store_split(mid_split, (slice(256, 512), cols), new_bottom)

    def first_cols(t):
        m, h = t // 2, t % 2
        band = slice(m * 512, m * 512 + 512)
        value = product(
            (mid_split[0, :, band], mid_split[1, :, band]), (fr_split[0, m, h], fr_split[1, m, h])
        )
        nxt[t] = value
        store_split(nxt_split, (t,), value)
        if t == 0:
            col_swaps[t] = send(nxt.at[0], from_right, col_prev)
        if t == 3:
            col_swaps[t] = send(nxt.at[3], from_left, col_next)

    def term(value, m, h, k):
        part = slice(k * 256, k * 256 + 256)
        return product(value, (sr_split[0, m, h, part], sr_split[1, m, h, part]))

    def kept(t):
        return nxt_split[0, t], nxt_split[1, t]

    def middle():
        for h in range(2):
            result[:, 256 + h * 256 : 512 + h * 256] = term(kept(1), 0, h, 0) + term(kept(2), 0, h, 1)

    def right_edge():
        edge = term(kept(3), 1, 0, 0)
        col_swaps[0].wait_recv()
        edge = edge + term(split(from_right[...]), 1, 0, 1)
        result[:, 768:] = jnp.where(col == 7, nxt[3], edge)

    def left_edge():
        edge = term(kept(0), 1, 1, 1)
        col_swaps[3].wait_recv()
        edge = edge + term(split(from_left[...]), 1, 1, 0)
        result[:, :256] = jnp.where(col == 0, nxt[0], edge)

    steps.update({"win": win_step, "mid": middle, "edgeR": right_edge, "edgeL": left_edge})
    for t in range(4):
        steps.update({
            "x1." + str(t): functools.partial(first_rows, t), "x2." + str(t): functools.partial(second_rows, t),
            "x3." + str(t): functools.partial(first_cols, t),
            "hop" + str(t): lambda t=t: border_pass(row_swaps[t]),
        })
    for name in ORDER:
        steps[name]()
    store = pltpu.make_async_copy(result, out, local_sem.at[len(loads)])
    store.start()
    for copy in sent:
        copy.wait_send()
    for copies in row_swaps.values():
        border_end(copies)

    @pl.when(core == 1)
    def _():
        at["shift"].wait_send()

    store.wait()


def shards(window, left_slots, right_slots, left_owner, right_owner):
    scratch = [
        pltpu.VMEM((512, 1024), F32),
        pltpu.VMEM((2, 512, 512), F32),
        pltpu.VMEM((2, 512, 512), F32),
        pltpu.VMEM((4, 512, 256), F32),
        pltpu.VMEM((4, 512, 256), F32),
        pltpu.VMEM((2, 512, 256), F32),
        pltpu.VMEM((2, 512, 256), F32),
        pltpu.VMEM((2, 2, 512, 256), F32),
        pltpu.VMEM((2, 2, 512, 256), F32),
        pltpu.VMEM((8, 6, HALF, 256), F32),
        pltpu.VMEM((8, 2, HALF, 256), F32),
        pltpu.VMEM((8, PIECE, 256), F32),
        pltpu.VMEM((4, PIECE, 256), F32),
        pltpu.VMEM((4, 4, HALF, 256), F32),
        pltpu.VMEM((4, 2, HALF, 256), F32),
        pltpu.VMEM((2, PIECE, 256), F32),
        pltpu.VMEM((2, 512, 1024), BF16),
        pltpu.VMEM((2, 2, 512, 256), BF16),
        pltpu.VMEM((2, 2, 512, 256), BF16),
        pltpu.VMEM((2, 2, 2, 512, 256), BF16),
        pltpu.VMEM((2, 2, 2, 512, 256), BF16),
        pltpu.VMEM((2, 512, 1024), BF16),
        pltpu.VMEM((4, 512, 256), F32),
        pltpu.VMEM((2, 4, 512, 256), BF16),
        pltpu.VMEM((4, 256, 256), F32),
        pltpu.VMEM((4, 256, 256), F32),
        pltpu.VMEM((4, 2, 128, 256), F32),
        pltpu.VMEM((4, 512, 256), F32),
        pltpu.VMEM((2, 4, 512, 256), BF16),
        pltpu.VMEM((512, 256), F32),
        pltpu.VMEM((512, 256), F32),
        pltpu.VMEM((512, 1024), F32),
        pltpu.SemaphoreType.DMA((COPIES,)),
        pltpu.SemaphoreType.DMA((COPIES,)),
        pltpu.SemaphoreType.DMA((8,)),
    ]
    smem, hbm = pl.BlockSpec(memory_space=pltpu.SMEM), pl.BlockSpec(memory_space=pl.ANY)
    return pl.pallas_call(
        kernel,
        name="far_update",
        out_shape=jax.ShapeDtypeStruct(window.shape, F32),
        in_specs=[smem, smem, hbm, hbm, hbm],
        out_specs=hbm,
        scratch_shapes=scratch,
        compiler_params=pltpu.CompilerParams(
            collective_id=0, has_side_effects=True, vmem_limit_bytes=58 * 2**20
        ),
    )(left_owner, right_owner, window, left_slots, right_slots)


def solution(mesh):
    in_specs = (
        P("row", "col"),
        P("row", "col", None, None, None, None),
        P("row", "col", None, None, None, None),
        P("row", None),
        P("col", None),
    )
    out_specs = P("row", "col")
    return jax.shard_map(shards, mesh=mesh, in_specs=in_specs, out_specs=out_specs, check_vma=False)
```

time: 475 us -> 95.5 us (0.20)
  waiting for transfers between devices: 386 us -> 0 us
  Pallas kernels: 0 us -> 91.9 us
  matrix products: 22.4 us -> 0 us
  local copies, waits for them, and re-layouts: 21.8 us -> 3.16 us
  between operations: 16 us -> 0.01 us
  starting transfers between devices: 12.9 us -> 0 us
  other arithmetic: 11.5 us -> 0 us
    psum x2 -> x0, waiting for transfers between devices: 337 us -> none  [spread(): return lax.psum(block, axis)]
    pallas_call x0 -> x1, Pallas kernels: none -> 91.9 us  [shards(): pl.pallas_call(kernel, name='far_update', out_shape=jax.ShapeDtypeStruct(...]
    ppermute x4 -> x0, waiting for transfers between devices: 48.6 us -> none  [shifted(): return lax.ppermute(block, axis, route)]
    dot_general x5 -> x0, matrix products: 22.4 us -> none  [the longest x3 12.2 us: right_apply(): return jnp.einsum('rmk,mkc->rmc', blocks, factors, precision=full_precision)]
    ppermute x4 -> x0, starting transfers between devices: 12.9 us -> none  [shifted(): return lax.ppermute(block, axis, route)]
    slice x7 -> x0, local copies, waits for them, and re-layouts: 10.9 us -> none  [the longest x2 5.26 us: shards(): first_right = spread(right_slots[0, 0, 0], 'row', right_owner[0, 0])]
    select_n x3 -> x0, other arithmetic: 5.36 us -> none  [the longest x1 2.56 us: spread(): jnp.where(lax.axis_index(axis) == source, block, jnp.zeros_like(block))]
    unnamed x10 -> x1, local copies, waits for them, and re-layouts: 8.07 us -> 3.16 us
  transfers between devices with their start and end apart: 6 -> 0, of which waited for: 6 -> 0; matrix products, arithmetic and copies ran while one was open for 7% -> 0% of each run, Pallas kernels for 0% -> 0%
where the time goes in v2:
time: 95.5 us; the launch traced here: 95.1 us
  Pallas kernels  91.9 us (96%)
  local copies, waits for them, and re-layouts  3.16 us (3%)
    pallas_call x1, Pallas kernels, shards(): pl.pallas_call(kernel, name='far_update', out_shape=jax.ShapeDtypeStruct(...  91.9 us
    unnamed x1, local copies, waits for them, and re-layouts  3.16 us

profile of v2, /device:TPU:1, one launch (start us, length us, event | category | flops | bytes accessed | tf_op | source)
XLA Modules:
  0.0 95.1 jit_solution(10458906121002431917)
XLA Ops:
  0.0 91.9 %far_update.1 = f32[512,1024]{1,0:T(8,128)} custom-call(s32[1,2]{1,0:T(1,128)} %left_owner.1, s32[1,2]{1,0:T(1,128)} %right_owner.1, f32[512,1024]{1,0:T(8,128)} %window.1, f32[1,1,2,1,512,512]{5,4,3,2,1,0:T(8,128)} %left.1, f32[1,1,2,2,512,512]{5,4,3,2,1,0:T(8,128)} %right.1), custom_call_target="tpu_custom_call" | custom-call | tf_op jit(solution)/shard_map/far_update/pallas_call | solution.py:558
  92.0 3.2 %copy.7 = f32[512,1024]{1,0:T(8,128)} copy(f32[512,1024]{1,0:T(8,128)} %far_update.1) | data formatting | bytes 4194304

commit v3 on v2

--- a/solution.py
+++ b/solution.py
@@ -12,16 +12,16 @@
 COPIES = 176
 PIECE, HALF = 128, 64
 ORDER = (
-    "L1a.start", "R1a.swap", "win", "R1b.swap", "R2a.swap", "L1b.start", "R1a.start", "L1a.merge",
-    "R1b.start", "L1b.merge", "L1a.home", "L2b.start", "R1a.merge", "L1b.home", "R1b.merge", "R2b.swap",
-    "L2a.start", "R1a.home", "R1b.home", "R2a.start", "L2b.merge", "R2b.start", "L1a.piece", "L2b.home",
-    "L1b.piece", "R1b.relay", "R2a.merge", "L2a.merge", "R2b.merge", "L1b.pass", "L1a.pass", "R1a.relay",
-    "L2b.shift", "R1b.piece", "L2a.home", "L2b.piece", "R2b.home", "R1a.piece", "L1b.done", "R1b.pass",
-    "L1a.done", "x1.0", "L2a.piece", "x1.1", "x1.2", "L2a.pass", "R2b.relay", "L2b.pass", "R1a.pass",
-    "R1b.last", "hop0", "x1.3", "hop1", "hop2", "R2a.home", "L2a.done", "L2b.done", "R1b.done", "x2.0",
-    "R2b.shift", "hop3", "x2.1", "R1a.last", "R2a.relay", "x2.2", "R2b.piece", "R1a.done", "x2.3", "x3.0",
-    "R2a.piece", "x3.3", "x3.2", "x3.1", "R2b.pass", "R2a.pass", "R2b.last", "R2a.last", "R2b.done",
-    "R2a.done", "mid", "edgeR", "edgeL",
+    "L1b.start", "R1b.swap", "win", "R1a.swap", "R2b.swap", "L1a.start", "R2a.swap", "R1b.start", "L1b.merge",
+    "R1a.start", "L1a.merge", "L1b.home", "L2b.start", "R1b.merge", "L1a.home", "R1a.merge", "R2b.start",
+    "L2a.start", "R1b.home", "L1b.piece", "R1a.home", "L2b.merge", "R2a.start", "R2b.merge", "R1b.relay",
+    "L2a.merge", "L1a.piece", "L1b.pass", "L2b.home", "R2a.merge", "R1a.relay", "R1b.piece", "L1a.pass",
+    "L2a.home", "L2b.shift", "R2b.home", "R1a.piece", "R1b.pass", "L1a.done", "L1b.done", "L2b.piece", "x1.0",
+    "L2a.piece", "R1b.last", "R2a.home", "x1.1", "hop0", "x1.2", "R1a.pass", "L2b.pass", "R1b.done",
+    "L2a.pass", "R2b.relay", "L2b.done", "x1.3", "hop1", "L2a.done", "hop2", "x2.0", "R1a.last", "R2a.relay",
+    "R2b.shift", "hop3", "x2.1", "R1a.done", "x3.0", "R2b.piece", "x2.2", "R2a.piece", "x2.3", "x3.3",
+    "R2b.pass", "R2a.pass", "R2b.last", "x3.2", "R2a.last", "x3.1", "R2b.done", "R2a.done", "mid", "edgeR",
+    "edgeL",
 )
 
 
@@ -176,12 +176,13 @@
         pair = (fl_split, sl_split)[s]
 
         def ref(where):
-            return left.at[0, 0, s, 0, where, here]
+            return left_own.at[s, where, here]
 
         def value(where):
             return left_own[s, where, here]
 
         def start():
+            need(load_left[s])
             at[f] = scatter_start(ref, x, xp, xm, f)
 
         def merge():
@@ -514,6 +515,19 @@
         at["shift"].wait_send()
 
     store.wait()
+
+
+def place(src, dst, held, in_sem, out_sem):
+    parts = [pl.ds(k * 64, 64) for k in range(8)]
+    reads = [pltpu.make_async_copy(src.at[p], held.at[p], in_sem.at[k]) for k, p in enumerate(parts)]
+    writes = [pltpu.make_async_copy(held.at[p], dst.at[p], out_sem.at[k]) for k, p in enumerate(parts)]
+    for copy in reads:
+        copy.start()
+    for read, write in zip(reads, writes):
+        read.wait()
+        write.start()
+    for copy in writes:
+        copy.wait()
 
 
 def shards(window, left_slots, right_slots, left_owner, right_owner):
@@ -555,7 +569,7 @@
         pltpu.SemaphoreType.DMA((8,)),
     ]
     smem, hbm = pl.BlockSpec(memory_space=pltpu.SMEM), pl.BlockSpec(memory_space=pl.ANY)
-    return pl.pallas_call(
+    made = pl.pallas_call(
         kernel,
         name="far_update",
         out_shape=jax.ShapeDtypeStruct(window.shape, F32),
@@ -566,6 +580,18 @@
             collective_id=0, has_side_effects=True, vmem_limit_bytes=58 * 2**20
         ),
     )(left_owner, right_owner, window, left_slots, right_slots)
+    return pl.pallas_call(
+        place,
+        name="place",
+        out_shape=jax.ShapeDtypeStruct(window.shape, F32),
+        in_specs=[hbm],
+        out_specs=hbm,
+        scratch_shapes=[
+            pltpu.VMEM(window.shape, F32),
+            pltpu.SemaphoreType.DMA((8,)),
+            pltpu.SemaphoreType.DMA((8,)),
+        ],
+    )(made)
 
 
 def solution(mesh):

time: 95.5 us -> 93.5 us (0.979)
  local copies, waits for them, and re-layouts: 3.16 us -> 0 us
  Pallas kernels: 91.9 us -> 93.3 us
    unnamed x1 -> x0, local copies, waits for them, and re-layouts: 3.16 us -> none
    pallas_call x0 -> x1, Pallas kernels: none -> 2.39 us  [shards(): pl.pallas_call(place, name='place', out_shape=jax.ShapeDtypeStruct(window...]
    pallas_call x1, Pallas kernels: 91.9 us -> 90.9 us  [shards(): pl.pallas_call(kernel, name='far_update', out_shape=jax.ShapeDtypeStruct(...]
where the time goes in v3:
time: 93.5 us; the launch traced here: 93.3 us
  Pallas kernels  93.3 us (100%)
    pallas_call x1, Pallas kernels, shards(): pl.pallas_call(kernel, name='far_update', out_shape=jax.ShapeDtypeStruct(...  90.9 us
    pallas_call x1, Pallas kernels, shards(): pl.pallas_call(place, name='place', out_shape=jax.ShapeDtypeStruct(window...  2.39 us

profile of v3, /device:TPU:1, one launch (start us, length us, event | category | flops | bytes accessed | tf_op | source)
XLA Modules:
  0.0 93.3 jit_solution(18163445552403562070)
XLA Ops:
  0.0 90.9 %far_update.1.src = f32[512,1024]{1,0:T(8,128)} custom-call(s32[1,2]{1,0:T(1,128)} %left_owner.1, s32[1,2]{1,0:T(1,128)} %right_owner.1, f32[512,1024]{1,0:T(8,128)} %window.1, f32[1,1,2,1,512,512]{5,4,3,2,1,0:T(8,128)} %left.1, f32[1,1,2,2,512,512]{5,4,3,2,1,0:T(8,128)} %right.1), custom_call_target="tpu_custom_call" | custom-call | tf_op jit(solution)/shard_map/far_update/pallas_call | solution.py:572
  90.9 2.4 %place.1 = f32[512,1024]{1,0:T(8,128)} custom-call(f32[512,1024]{1,0:T(8,128)} %far_update.1.src), custom_call_target="tpu_custom_call" | custom-call | tf_op jit(solution)/shard_map/place/pallas_call | solution.py:583

commit v4 on v3

--- a/solution.py
+++ b/solution.py
@@ -41,7 +41,7 @@
 
 def kernel(
     left_owner, right_owner, window, left, right, out,
-    win, left_own, right_own, right_swap, right_pick,
+    win, left_own, right_own, right_give, right_swap, right_pick,
     first_left, second_left, first_right, second_right,
     arrive, merged, home, left_z, right_z, relay, aside,
     win_split, fl_split, sl_split, fr_split, sr_split,
@@ -72,6 +72,7 @@
         return copy
 
     load_left = [load(left.at[0, 0, s, 0], left_own.at[s]) for s in range(2)]
+    load_give = [load(right.at[0, 0, s, 1 - core], right_give.at[s]) for s in range(2)]
     load_right = [load(right.at[0, 0, s, core], right_own.at[s]) for s in range(2)]
     load_win = load(window, win)
     loaded = []
@@ -235,7 +236,8 @@
             return right_pick[g, where, :]
 
         def swap():
-            at[f] = send(right.at[0, 0, s, 1 - core, :, here], right_swap.at[g], mate)
+            need(load_give[s])
+            at[f] = send(right_give.at[s, :, here], right_swap.at[g], mate)
 
         def start():
             need(load_right[s])
@@ -533,6 +535,7 @@
 def shards(window, left_slots, right_slots, left_owner, right_owner):
     scratch = [
         pltpu.VMEM((512, 1024), F32),
+        pltpu.VMEM((2, 512, 512), F32),
         pltpu.VMEM((2, 512, 512), F32),
         pltpu.VMEM((2, 512, 512), F32),
         pltpu.VMEM((4, 512, 256), F32),

time: 93.5 us -> 93.4 us (level)
  no operation moved by 1% of the time
where the time goes in v4:
time: 93.4 us; the launch traced here: 93.3 us
  Pallas kernels  93.3 us (100%)
    pallas_call x1, Pallas kernels, shards(): pl.pallas_call(kernel, name='far_update', out_shape=jax.ShapeDtypeStruct(...  90.9 us
    pallas_call x1, Pallas kernels, shards(): pl.pallas_call(place, name='place', out_shape=jax.ShapeDtypeStruct(window...  2.39 us

profile of v4, /device:TPU:1, one launch (start us, length us, event | category | flops | bytes accessed | tf_op | source)
XLA Modules:
  0.0 93.3 jit_solution(12248659309551382052)
XLA Ops:
  0.0 90.9 %far_update.1.src = f32[512,1024]{1,0:T(8,128)} custom-call(s32[1,2]{1,0:T(1,128)} %left_owner.1, s32[1,2]{1,0:T(1,128)} %right_owner.1, f32[512,1024]{1,0:T(8,128)} %window.1, f32[1,1,2,1,512,512]{5,4,3,2,1,0:T(8,128)} %left.1, f32[1,1,2,2,512,512]{5,4,3,2,1,0:T(8,128)} %right.1), custom_call_target="tpu_custom_call" | custom-call | tf_op jit(solution)/shard_map/far_update/pallas_call | solution.py:575
  90.9 2.4 %place.1 = f32[512,1024]{1,0:T(8,128)} custom-call(f32[512,1024]{1,0:T(8,128)} %far_update.1.src), custom_call_target="tpu_custom_call" | custom-call | tf_op jit(solution)/shard_map/place/pallas_call | solution.py:586
